TPU v7x, 512 devices: a whole 4x4x16 slice. The times are simulated.
512 devices in a mesh: seq: 16 (over z), ch: 32 (over x, y, core).
Axes of the slice: x: 4, y: 4, z: 16, core: 2. Of those that a mesh axis runs over, the one named last changes fastest.
Arguments:
- inputs: bfloat16 [4096, 8192], P('seq', 'ch'), may hold values from -6 to 6
- w_in: bfloat16 [3, 8192, 8192], P(None, 'seq', 'ch'), may hold values from -0.0625 to 0.0625
- short_filter: float32 [3, 3, 8192], P(None, None, 'ch'), may hold values from -3 to 3
- rates: float32 [16, 8192], P(None, 'ch'), may hold values from 2.4414063e-05 to 0.05
- residues: float32 [16, 8192], P(None, 'ch'), may hold values from -3 to 3
- skip: float32 [8192], P('ch'), may hold values from -3 to 3
Outputs:
- gated: bfloat16 [4096, 8192], P('seq', 'ch')
All inputs are finite; a program needn't handle non-finite values.
Results may differ from a plain program's by a relative error of at most 0.0065.
Values may be sent and summed in bfloat16 or wider, within the bound.
A program may use at most 64 MiB of HBM per device.

v0:
```python
import jax
import jax.numpy as jnp
from jax import lax
from jax.sharding import PartitionSpec as P

TAPS = 3


def passed_along(block, axis, distance):
    devices = range(lax.axis_size(axis))
    route = [(i - distance, i) for i in devices if i - distance in devices]
    return lax.ppermute(block, axis, route)


def carried_in(part, axis, combine, identity):
    place = lax.axis_index(axis)
    gathered = jax.tree.map(lambda a: lax.all_gather(a, axis), part)
    state = jax.tree.map(lambda a, e: jnp.zeros_like(a) + jnp.asarray(e, a.dtype), part, identity)

    def one(hop, state):
        return combine(
            state, jax.tree.map(lambda a: lax.dynamic_index_in_dim(a, hop, 0, False), gathered)
        )

    return lax.fori_loop(0, place, one, state)


def combine(earlier, later):
    return (earlier[0] * later[0], earlier[1] * later[0] + later[1])


def per_device(inputs, w_in, short_filter, rates, residues, skip):
    tok_rows = inputs.shape[0]
    width = w_in.shape[2]
    modes = rates.shape[0]
    features = lax.all_gather(inputs, "ch", axis=1, tiled=True)
    proj = jnp.einsum(
        "td,kdc->ktc",
        features,
        lax.all_gather(w_in, "seq", axis=1, tiled=True),
        preferred_element_type=jnp.float32,
    ).astype(jnp.bfloat16)
    prior = passed_along(proj[:, tok_rows - (TAPS - 1) :, :], "seq", 1)
    padded = jnp.concatenate([prior, proj], axis=1).astype(jnp.float32)
    mixed = jnp.zeros((3, tok_rows, width), jnp.float32)
    for j in range(TAPS):
        mixed = (
            mixed
            + short_filter[:, j, None, :] * padded[:, TAPS - 1 - j : TAPS - 1 - j + tok_rows, :]
        )
    query, key, value = (mixed[0], mixed[1], mixed[2])
    drive = key * value
    position = jnp.arange(tok_rows, dtype=jnp.float32)
    scaled = residues * jnp.sqrt(1.0 - jnp.exp(-2.0 * rates))
    end_powers = jnp.exp(-rates[None, :, :] * (tok_rows - 1.0 - position)[:, None, None])
    end_state = jnp.sum(end_powers * drive[:, None, :], axis=0)
    block_decay = jnp.exp(-rates * tok_rows)
    identity = (jnp.ones_like(block_decay), jnp.zeros_like(end_state))
    entering = carried_in((block_decay, end_state), "seq", combine, identity)[1]
    start_powers = jnp.exp(-rates[None, :, :] * (position + 1.0)[:, None, None])
    cross = jnp.sum(start_powers * (scaled * entering)[None, :, :], axis=1)
    center = (tok_rows - 1.0) / 2.0
    offset = (position - center)[:, None, None]
    rising = jnp.exp(rates[None, :, :] * offset) * drive[:, None, :]
    offsets = jnp.arange(tok_rows, dtype=jnp.int32)
    lower = (offsets[:, None] >= offsets[None, :]).astype(jnp.float32)
    prefix = jnp.dot(
        lower, rising.reshape(tok_rows, modes * width), precision=lax.Precision.HIGHEST
    )
    prefix = prefix.reshape(tok_rows, modes, width)
    falling = jnp.exp(-rates[None, :, :] * offset) * scaled[None, :, :]
    local = jnp.sum(falling * prefix, axis=1)
    return (query * (local + cross + skip[None, :] * drive)).astype(jnp.bfloat16)


def solution(mesh):
    in_specs = (
        P("seq", "ch"),
        P(None, "seq", "ch"),
        P(None, None, "ch"),
        P(None, "ch"),
        P(None, "ch"),
        P("ch"),
    )
    out_specs = P("seq", "ch")
    return jax.shard_map(
        per_device, mesh=mesh, in_specs=in_specs, out_specs=out_specs, check_vma=False
    )
```

profile of v0, /device:TPU:24, one launch (start us, length us, event | category | flops | bytes accessed | tf_op | source)
XLA Modules:
  0.0 286.4 jit_solution(2739463893934108773)
XLA Ops:
  6.5 0.0 all-gather.7.cloned.1.call-start
  6.5 0.7 all-gather.7.cloned.1.call-update
  7.3 0.0 all-gather.5.cloned.1.call-start
  7.3 0.7 all-gather.5.cloned.1.call-update
  8.0 0.7 fusion.16
  8.8 36.8 %all-gather = f32[256,256]{1,0:T(8,128)S(1)} all-gather(f32[16,256]{1,0:T(8,128)S(1)} %get-tuple-element.63), channel_id=2, replica_groups=mesh['seq'=16,'ch'=32] {'seq'}, dimensions={0}, use_global_device_ids=true | all-gather | bytes 278528 | tf_op jit(solution)/shard_map/all_gather | solution.py:17
  45.6 0.8 fusion.17
  46.4 0.0 copy-start
  46.4 32.4 %all-gather.7.cloned.1.call-done = bf16[256,8192]{1,0:T(8,128)(2,1)} async-done(((bf16[256,256]{1,0:T(8,128)(2,1)}), bf16[256,8192]{1,0:T(8,128)(2,1)}) %all-gather.7.cloned.1.call-update) | async-done | bytes 4194320 | tf_op jit(solution)/shard_map/all_gather | solution.py:36
  78.8 150.2 %all-gather.5.cloned.1.call-done = bf16[3,8192,256]{2,1,0:T(8,128)(2,1)} async-done(((bf16[3,512,256]{2,1,0:T(8,128)(2,1)}), bf16[3,8192,256]{2,1,0:T(8,128)(2,1)}) %all-gather.5.cloned.1.call-update) | async-done | bytes 12582928 | tf_op jit(solution)/shard_map/all_gather | solution.py:40
  229.0 9.3 %fusion.5 = bf16[3,256,256]{2,1,0:T(8,128)(2,1)S(1)} fusion(bf16[3,8192,256]{2,1,0:T(8,128)(2,1)} %all-gather.5.cloned.1.call-done, bf16[256,8192]{1,0:T(8,128)(2,1)} %all-gather.7.cloned.1.call-done), kind=kOutput, calls=%fused_computation.9 | convolution fusion | flops 3221422080 | bytes 17170432 | tf_op jit(solution)/shard_map/td,kdc->ktc/dot_general | solution.py:37
  238.3 1.3 collective-permute-start
  239.6 0.0 copy-done
  239.7 0.0 copy-start.1
  239.7 1.2 collective-permute-done
  240.9 0.1 maximum_convert_fusion
  241.0 0.2 fusion.8
  241.3 0.1 copy.12
  241.4 0.8 multiply_reduce_fusion.1
  242.2 31.9 %all-gather.1 = f32[256,256]{1,0:T(8,128)S(1)} all-gather(f32[16,256]{1,0:T(8,128)S(1)} %multiply_reduce_fusion.1), channel_id=3, replica_groups=mesh['seq'=16,'ch'=32] {'seq'}, dimensions={0}, use_global_device_ids=true | all-gather | bytes 278528 | tf_op jit(solution)/shard_map/all_gather | solution.py:17
  274.1 0.0 copy-done.1
  274.2 0.6 bitcast_multiply_fusion.1
  274.8 0.0 copy-start.2
  274.8 3.2 %multiply_reduce_fusion.2 = f32[256,256]{1,0:T(8,128)S(1)} fusion(f32[16,256,256]{2,1,0:T(8,128)S(1)} %bitcast.50, f32[16,256]{1,0:T(8,128)S(1)} %get-tuple-element.61, f32[256]{0:T(256)S(1)} %iota_add_fusion.1, f32[16,256]{1,0:T(8,128)S(1)} %get-tuple-element.62), kind=kOutput, calls=%fused_computation.7 | convolution fusion | flops 3225419776 | bytes 4490240 | tf_op jit(solution)/shard_map/dot_general | solution.py:67
  278.0 0.7 multiply_reduce_fusion
  278.8 0.0 copy-done.2
  278.8 0.7 fusion.12
  (11 shorter events, 0.1 us)
Async XLA Ops:
  6.5 72.3 %all-gather.7.cloned.1.call-start = ((), (), s32[]{:S(2)}) async-start(), calls=%async_computation.1 | async-start | bytes 4325376 | tf_op jit(solution)/shard_map/all_gather | solution.py:36
  7.3 221.8 %all-gather.5.cloned.1.call-start = ((), (), s32[]{:S(2)}) async-start(), calls=%async_computation | async-start | bytes 13369344 | tf_op jit(solution)/shard_map/all_gather | solution.py:40
  46.4 193.2 %copy-start = (f32[16,256]{1,0:T(8,128)S(1)}, f32[16,256]{1,0:T(8,128)}, u32[]{:S(2)}) copy-start(f32[16,256]{1,0:T(8,128)} %param.11) | copy-start | bytes 49156
  238.3 2.6 collective-permute-start
  239.7 34.5 %copy-start.1 = (f32[16,256]{1,0:T(8,128)S(1)}, f32[16,256]{1,0:T(8,128)}, u32[]{:S(2)}) copy-start(f32[16,256]{1,0:T(8,128)} %param.12) | copy-start | bytes 49156
  274.8 4.0 %copy-start.2 = (f32[256]{0:T(256)S(1)}, f32[256]{0:T(256)}, u32[]{:S(2)}) copy-start(f32[256]{0:T(256)} %param.13) | copy-start | bytes 3076
Sparse Core Ops, SparseCore 0:
  10.4 68.3 all-gather.6
  80.9 148.0 all-gather.4
where the time goes:
time: 287 us; the launch traced here: 286 us
  waiting for transfers between devices  185 us (64%)
  blocking collectives  68.7 us (24%)
  between operations  13.6 us (5%)
  matrix products  12.5 us (4%)
  other arithmetic  4.02 us (1%)
    all_gather x1, waiting for transfers between devices, per_device(): lax.all_gather(w_in, 'seq', axis=1, tiled=True)  150 us
    all_gather x2, blocking collectives, carried_in(): gathered = jax.tree.map(lambda a: lax.all_gather(a, axis), part)  68.7 us
    all_gather x1, waiting for transfers between devices, per_device(): features = lax.all_gather(inputs, 'ch', axis=1, tiled=True)  32.4 us
    dot_general x1, matrix products, per_device(): jnp.einsum('td,kdc->ktc', features, lax.all_gather(w_in, 'seq', axis=1, t...  9.25 us
  transfers between devices with their start and end apart: 3, of which 3 were waited for; matrix products, arithmetic and copies ran while one was open for 1% of the time, Pallas kernels for 0%

commit v1 on v0

v1 whole, which is shorter than its diff:
```python
import functools

import jax
import jax.numpy as jnp
from jax import lax
from jax.experimental import pallas as pl
from jax.experimental.pallas import tpu as pltpu
from jax.sharding import PartitionSpec as P

MESH = pl.DeviceIdType.MESH
Z = 16
S = 4
TOK = 256
LANE = 128
MODES = 16
TAPS = 3


def kernel(
    x_ref, w_ref, sf_ref, rates_ref, res_ref, skip_ref, out_ref,
    wg, xg, acc, pad, halo, query, drive, est, ysum,
    xy_s, xy_r, xx_s, xx_r, xc_s, xc_r, w_s, w_r, h_s, h_r, e_s, e_r,
):
    z = lax.axis_index("seq")
    ch = lax.axis_index("ch")
    core = ch % 2
    y = (ch // 2) % S
    x = ch // (2 * S)
    c = ch // 2

    def z_at(d):
        return ((z + d) % Z, ch)

    def y_at(d):
        return (z, (x * S + (y + d) % S) * 2 + core)

    def x_at(d):
        return (z, (((x + d) % S) * S + y) * 2 + core)

    other = (z, c * 2 + 1 - core)

    barrier = pltpu.get_barrier_semaphore()
    partners = [z_at(d) for d in range(1, Z)] + [y_at(d) for d in range(1, S)]
    partners += [x_at(d) for d in range(1, S)] + [other]
    for p in partners:
        pl.semaphore_signal(barrier, inc=1, device_id=p, device_id_type=MESH)
    pl.semaphore_wait(barrier, len(partners))

    started = []

    def remote(src, dst, ss, rs, dev):
        return pltpu.make_async_remote_copy(
            src_ref=src, dst_ref=dst, send_sem=ss, recv_sem=rs, device_id=dev, device_id_type=MESH
        )

    def go(copy):
        copy.start()
        started.append(copy)

    def valid(way, k, p):
        return k < Z // 2 or p == way

    def slot(way, h, k, p):
        return wg.at[h, (z - k if way == 0 else z + k) % Z, p]

    def w_copy(way, h, k, p, at):
        ref = slot(way, h, at, p)
        return remote(ref, ref, w_s.at[way, h, k, p], w_r.at[way, h, k, p], z_at(1 if way == 0 else -1))

    def own(h):
        for p in range(2):
            wg[h, z, p] = w_ref[:, pl.ds(256 * p, 256), pl.ds(LANE * h, LANE)]

    def inject(h):
        for p in range(2):
            for way in range(2):
                go(w_copy(way, h, 0, p, 0))

    own(0)
    inject(0)
    xg[core, c] = x_ref[...]
    for d in range(1, S):
        go(remote(xg.at[core, c], xg.at[core, c], xy_s.at[d - 1], xy_r.at[d - 1], y_at(d)))
    own(1)

    def x_second():
        for d in range(1, S):
            ref = xg.at[core, x * S + (y - d) % S]
            remote(ref, ref, xy_s.at[d - 1], xy_r.at[d - 1], y_at(d)).wait_recv()
        mine = xg.at[core, pl.ds(x * S, S)]
        for d in range(1, S):
            go(remote(mine, mine, xx_s.at[d - 1], xx_r.at[d - 1], x_at(d)))
        go(remote(mine, mine, xc_s.at[0], xc_r.at[0], other))

    def x_third():
        for d in range(1, S):
            ref = xg.at[core, pl.ds(((x - d) % S) * S, S)]
            remote(ref, ref, xx_s.at[d - 1], xx_r.at[d - 1], x_at(d)).wait_recv()
            go(remote(ref, ref, xc_s.at[d], xc_r.at[d], other))

    def x_last():
        for d in range(S):
            ref = xg.at[1 - core, pl.ds(((x - d) % S) * S, S)]
            remote(ref, ref, xc_s.at[d], xc_r.at[d], other).wait_recv()

    def project(h):
        acc[...] = jnp.zeros_like(acc)

        @pl.loop(0, Z)
        def _(s):
            for i in range(3):
                total = acc[i]
                for p in range(2):
                    total += jnp.dot(xg[p, s], wg[h, s, p, i], preferred_element_type=jnp.float32)
                acc[i] = total

    def halo_copy(h):
        return remote(pad.at[h, :, pl.ds(TOK, 8)], halo.at[h], h_s.at[h], h_r.at[h], z_at(1))

    def part1(h):
        for i in range(3):
            pad[h, i, 8:, :] = acc[i].astype(jnp.bfloat16).astype(jnp.float32)
        go(halo_copy(h))

    def lanes(h):
        return pl.ds(LANE * h, LANE)

    def state_copy(h, d, src, to):
        return remote(est.at[h, src], est.at[h, src], e_s.at[h, d - 1], e_r.at[h, d - 1], to)

    def part2(h):
        halo_copy(h).wait_recv()
        first = (z > 0).astype(jnp.float32)
        mixed = []
        for i in range(3):
            pad[h, i, 0:8, :] = halo[h, i] * first
            total = jnp.zeros((TOK, LANE), jnp.float32)
            for j in range(TAPS):
                total += sf_ref[i, pl.ds(j, 1), lanes(h)] * pad[h, i, 8 - j : 8 - j + TOK, :]
            mixed.append(total)
        query[h] = mixed[0]
        drive[h] = mixed[1] * mixed[2]
        r = rates_ref[:, lanes(h)]
        f8 = jnp.exp(-8.0 * r)
        steps = [jnp.broadcast_to(f8[m : m + 1, :], (8, LANE)) for m in range(MODES)]

        def one(g, states):
            d = drive[h, pl.ds(pl.multiple_of(g * 8, 8), 8), :]
            return tuple(s * f + d for s, f in zip(states, steps))

        states = lax.fori_loop(0, TOK // 8, one, tuple(jnp.zeros((8, LANE), jnp.float32) for _ in range(MODES)))
        left = 7.0 - lax.broadcasted_iota(jnp.int32, (8, LANE), 0).astype(jnp.float32)
        for m in range(MODES):
            weight = jnp.exp(-r[m : m + 1, :] * left)
            est[h, z, pl.ds(m, 1), :] = jnp.sum(states[m] * weight, axis=0, keepdims=True)
        for d in range(1, Z):
            go(state_copy(h, d, z, z_at(d)))

    def part3(h):
        for d in range(1, Z):
            state_copy(h, d, (z - d) % Z, z_at(d)).wait_recv()
        r = rates_ref[:, lanes(h)]
        block = jnp.exp(-float(TOK) * r)
        entering = jnp.zeros((MODES, LANE), jnp.float32)
        for s in range(Z - 1):
            entering = jnp.where(s < z, entering * block + est[h, s], entering)
        factor = jnp.exp(-r)
        scaled = res_ref[:, lanes(h)] * jnp.sqrt(1.0 - jnp.exp(-2.0 * r))
        fa, fb, sa, sb = factor[:8], factor[8:], scaled[:8], scaled[8:]

        def one(g, state):
            a, b = state
            base = pl.multiple_of(g * 8, 8)
            for t in range(8):
                d = drive[h, pl.ds(base + t, 1), :]
                a = a * fa + d
                b = b * fb + d
                ysum[pl.ds(pl.multiple_of((base + t) * 8, 8), 8), :] = a * sa + b * sb
            return a, b

        lax.fori_loop(0, TOK // 8, one, (entering[:8], entering[8:]))
        total = ysum[pl.ds(0, TOK, stride=8), :]
        for i in range(1, 8):
            total += ysum[pl.ds(i, TOK, stride=8), :]
        gated = query[h] * (total + skip_ref[:, lanes(h)] * drive[h])
        out_ref[:, lanes(h)] = gated.astype(jnp.bfloat16)

    for step in range(Z):
        h, k = step // (Z // 2), step % (Z // 2) + 1
        for p in range(2):
            for way in range(2):
                if valid(way, k, p):
                    w_copy(way, h, k - 1, p, k).wait_recv()
                    if k < Z // 2 and valid(way, k + 1, p):
                        go(w_copy(way, h, k, p, k))
        if h == 0 and k == Z // 2 - 1:
            inject(1)
        if step == 0:
            x_second()
        if step == 4:
            x_third()
        if step == 5:
            x_last()
        if step == 7:
            project(0)
            part1(0)
        if step == 9:
            part2(0)
        if step == 11:
            part3(0)
    project(1)
    part1(1)
    part2(1)
    part3(1)
    for copy in started:
        copy.wait_send()


def per_device(inputs, w_in, short_filter, rates, residues, skip):
    vmem = pl.BlockSpec(memory_space=pltpu.VMEM)
    dma = pltpu.SemaphoreType.DMA
    f32, bf16 = jnp.float32, jnp.bfloat16
    return pl.pallas_call(
        kernel,
        out_shape=jax.ShapeDtypeStruct(inputs.shape, jnp.bfloat16),
        in_specs=[vmem] * 6,
        out_specs=vmem,
        scratch_shapes=[
            pltpu.VMEM((2, Z, 2, 3, 256, LANE), bf16),
            pltpu.VMEM((2, 16, TOK, 256), bf16),
            pltpu.VMEM((3, TOK, LANE), f32),
            pltpu.VMEM((2, 3, TOK + 8, LANE), f32),
            pltpu.VMEM((2, 3, 8, LANE), f32),
            pltpu.VMEM((2, TOK, LANE), f32),
            pltpu.VMEM((2, TOK, LANE), f32),
            pltpu.VMEM((2, Z, MODES, LANE), f32),
            pltpu.VMEM((TOK * 8, LANE), f32),
            dma((3,)), dma((3,)), dma((3,)), dma((3,)), dma((4,)), dma((4,)),
            dma((2, 2, 8, 2)), dma((2, 2, 8, 2)), dma((2,)), dma((2,)),
            dma((2, Z - 1)), dma((2, Z - 1)),
        ],
        compiler_params=pltpu.CompilerParams(
            collective_id=0, has_side_effects=True, vmem_limit_bytes=48 * 2**20
        ),
    )(inputs, w_in, short_filter, rates, residues, skip.reshape(1, -1))


def solution(mesh):
    in_specs = (
        P("seq", "ch"),
        P(None, "seq", "ch"),
        P(None, None, "ch"),
        P(None, "ch"),
        P(None, "ch"),
        P("ch"),
    )
    return jax.shard_map(
        per_device, mesh=mesh, in_specs=in_specs, out_specs=P("seq", "ch"), check_vma=False
    )
```

time: 287 us -> 178 us (0.62)
  waiting for transfers between devices: 185 us -> 0 us
  Pallas kernels: 0 us -> 172 us
  blocking collectives: 68.7 us -> 0 us
  between operations: 13.6 us -> 0.02 us
  matrix products: 12.5 us -> 0 us
  local copies, waits for them, and re-layouts: 1 us -> 5.51 us
  other arithmetic: 4.02 us -> 0 us
    all_gather x2 -> x0, waiting for transfers between devices: 183 us -> none  [the longest x1 150 us: per_device(): lax.all_gather(w_in, 'seq', axis=1, tiled=True)]
    pallas_call x0 -> x1, Pallas kernels: none -> 172 us  [per_device(): pl.pallas_call(kernel, out_shape=jax.ShapeDtypeStruct(inputs.shape, jnp.b...]
    all_gather x2 -> x0, blocking collectives: 68.7 us -> none  [carried_in(): gathered = jax.tree.map(lambda a: lax.all_gather(a, axis), part)]
    dot_general x2 -> x0, matrix products: 12.5 us -> none  [the longest x1 9.25 us: per_device(): jnp.einsum('td,kdc->ktc', features, lax.all_gather(w_in, 'seq', axis=1, t...]
    unnamed x10 -> x13, local copies, waits for them, and re-layouts: 0.16 us -> 5.51 us
  transfers between devices with their start and end apart: 3 -> 0, of which waited for: 3 -> 0; matrix products, arithmetic and copies ran while one was open for 1% -> 0% of each run, Pallas kernels for 0% -> 0%
where the time goes in v1:
time: 178 us; the launch traced here: 177 us
  Pallas kernels  172 us (97%)
  local copies, waits for them, and re-layouts  5.51 us (3%)
    pallas_call x1, Pallas kernels, per_device(): pl.pallas_call(kernel, out_shape=jax.ShapeDtypeStruct(inputs.shape, jnp.b...  172 us
    unnamed x13, local copies, waits for them, and re-layouts  5.51 us

profile of v1, /device:TPU:24, one launch (start us, length us, event | category | flops | bytes accessed | tf_op | source)
XLA Modules:
  0.0 177.5 jit_solution(10999446283309419265)
XLA Ops:
  0.0 0.0 copy-start.5
  0.0 0.7 copy-done.5
  0.7 0.0 copy-start
  0.7 1.1 copy-done
  1.8 0.0 copy-start.1
  1.8 0.9 copy-done.1
  2.7 0.0 copy-start.2
  2.7 0.7 copy-done.2
  3.4 0.0 copy-start.3
  3.4 0.7 copy-done.3
  4.2 0.0 copy-start.4
  4.2 0.7 copy-done.4
  4.9 171.9 %shard_map.64 = bf16[256,256]{1,0:T(8,128)(2,1)S(1)} custom-call(bf16[256,256]{1,0:T(8,128)(2,1)S(1)} %copy-done.1, bf16[3,512,256]{2,1,0:T(8,128)(2,1)S(1)} %copy-done, f32[3,3,256]{2,1,0:T(4,128)S(1)} %copy-done.4, f32[16,256]{1,0:T(8,128)S(1)} %copy-done.2, f32[16,256]{1,0:T(8,128)S(1)} %copy-done.3, f32[1,256]{1,0:T(1,128)S(1)} %bitcast.1), custom_call_target="tpu_custom_call" | custom-call | tf_op jit(solution)/shard_map/pallas_call | solution.py:223
  176.8 0.7 copy.8
Async XLA Ops:
  0.0 0.7 copy-start.5
  0.7 1.1 copy-start
  1.8 0.9 copy-start.1
  2.7 0.7 copy-start.2
  3.4 0.7 copy-start.3
  4.2 0.7 copy-start.4

commit v2 on v1

--- a/solution.py
+++ b/solution.py
@@ -16,10 +16,30 @@
 TAPS = 3
 
 
+CHUNKS = ((0, 2), (2, 2), (4, 4), (8, 4), (12, 4))
+SCALE = 2.0**16
+
+
+def need_slot(tau):
+    ahead = (tau - 1) % Z + 1
+    late = (ahead - 1) // (Z // 2)
+    return (1 - late) * (Z - 2 * ahead) + late * (2 * ahead - Z - 1)
+
+
+def coded(total):
+    return (total * jnp.abs(total) * (total * total)).astype(jnp.bfloat16)
+
+
+def plain(sent):
+    fourth = sent.astype(jnp.float32)
+    root = lax.rsqrt(jnp.maximum(jnp.abs(fourth), 1e-37))
+    return fourth * root * root * lax.rsqrt(root)
+
+
 def kernel(
     x_ref, w_ref, sf_ref, rates_ref, res_ref, skip_ref, out_ref,
-    wg, xg, acc, pad, halo, query, drive, est, ysum,
-    xy_s, xy_r, xx_s, xx_r, xc_s, xc_r, w_s, w_r, h_s, h_r, e_s, e_r,
+    xs, xg, ring, part, acc, pad, halo, query, drive, est, ysum,
+    sc_s, sc_r, xy_s, xy_r, xx_s, xx_r, xc_s, xc_r, p_s, p_r, h_s, h_r, e_s, e_r,
 ):
     z = lax.axis_index("seq")
     ch = lax.axis_index("ch")
@@ -38,13 +58,23 @@
         return (z, (((x + d) % S) * S + y) * 2 + core)
 
     other = (z, c * 2 + 1 - core)
-
     barrier = pltpu.get_barrier_semaphore()
+
+    def greet(device):
+        pl.semaphore_signal(barrier, inc=1, device_id=device, device_id_type=MESH)
+
     partners = [z_at(d) for d in range(1, Z)] + [y_at(d) for d in range(1, S)]
     partners += [x_at(d) for d in range(1, S)] + [other]
+    partners += [((z + d) % Z, z * 2 + core) for d in range(1, Z)]
     for p in partners:
-        pl.semaphore_signal(barrier, inc=1, device_id=p, device_id_type=MESH)
-    pl.semaphore_wait(barrier, len(partners))
+        greet(p)
+
+    @pl.when(c != z)
+    def _():
+        greet((z, z * 2 + core))
+
+    xs[...] = x_ref[...] * jnp.bfloat16(SCALE)
+    pl.semaphore_wait(barrier, len(partners) + (c != z).astype(jnp.int32))
 
     started = []
 
@@ -57,69 +87,126 @@
         copy.start()
         started.append(copy)
 
-    def valid(way, k, p):
-        return k < Z // 2 or p == way
-
-    def slot(way, h, k, p):
-        return wg.at[h, (z - k if way == 0 else z + k) % Z, p]
-
-    def w_copy(way, h, k, p, at):
-        ref = slot(way, h, at, p)
-        return remote(ref, ref, w_s.at[way, h, k, p], w_r.at[way, h, k, p], z_at(1 if way == 0 else -1))
-
-    def own(h):
-        for p in range(2):
-            wg[h, z, p] = w_ref[:, pl.ds(256 * p, 256), pl.ds(LANE * h, LANE)]
-
-    def inject(h):
-        for p in range(2):
+    def scatter(d):
+        to = (c + d) % Z
+        rows = pl.ds(pl.multiple_of(to * 16, 16), 16)
+        r = need_slot((z - c) % Z)
+        return remote(xs.at[rows], xg.at[core, r, rows], sc_s.at[d], sc_r.at[r], (c, to * 2 + core))
+
+    for d in range(1, Z):
+        go(scatter(d))
+
+    @pl.when(c != z)
+    def _():
+        scatter(0).start()
+
+    mine = pl.ds(pl.multiple_of(c * 16, 16), 16)
+
+    @pl.when(c == z)
+    def _():
+        xg[core, Z - 1, mine] = xs[mine]
+
+    def scattered(r):
+        ref = xg.at[core, r, mine]
+        remote(ref, ref, sc_s.at[0], sc_r.at[r], other).wait_recv()
+
+    def bundle(which, n, at, rows):
+        first, count = CHUNKS[n]
+        return xg.at[which, pl.ds(first, count), pl.ds(pl.multiple_of(at * rows, 16), rows)]
+
+    def x_first(n):
+        first, count = CHUNKS[n]
+        for r in range(first, first + count):
+            if r == Z - 1:
+                @pl.when(c != z)
+                def _():
+                    scattered(r)
+            else:
+                scattered(r)
+        ref = bundle(core, n, c, 16)
+        for d in range(1, S):
+            go(remote(ref, ref, xy_s.at[n, d - 1], xy_r.at[n, d - 1], y_at(d)))
+
+    def x_second(n):
+        for d in range(1, S):
+            ref = bundle(core, n, x * S + (y - d) % S, 16)
+            remote(ref, ref, xy_s.at[n, d - 1], xy_r.at[n, d - 1], y_at(d)).wait_recv()
+        ref = bundle(core, n, x, 64)
+        for d in range(1, S):
+            go(remote(ref, ref, xx_s.at[n, d - 1], xx_r.at[n, d - 1], x_at(d)))
+        go(remote(ref, ref, xc_s.at[n, 0], xc_r.at[n, 0], other))
+
+    def x_third(n):
+        for d in range(1, S):
+            ref = bundle(core, n, (x - d) % S, 64)
+            remote(ref, ref, xx_s.at[n, d - 1], xx_r.at[n, d - 1], x_at(d)).wait_recv()
+            go(remote(ref, ref, xc_s.at[n, d], xc_r.at[n, d], other))
+
+    def x_last(n):
+        for d in range(S):
+            ref = bundle(1 - core, n, (x - d) % S, 64)
+            remote(ref, ref, xc_s.at[n, d], xc_r.at[n, d], other).wait_recv()
+
+    def sends(way, h):
+        return Z // 2 if way == h else Z // 2 - 1
+
+    def product(r, h, i):
+        total = jnp.dot(xg[0, r], w_ref[i, 0:256, lanes(h)], preferred_element_type=jnp.float32)
+        return total + jnp.dot(xg[1, r], w_ref[i, 256:512, lanes(h)], preferred_element_type=jnp.float32)
+
+    def hop(way, h, j, i):
+        return remote(
+            ring.at[h, way, j, i], ring.at[h, way, j + 1, i],
+            p_s.at[h, way, j, i], p_r.at[h, way, j, i], z_at(1 - 2 * way),
+        )
+
+    def arrived(way, h, j, i):
+        ref = ring.at[h, way, j, i]
+        remote(ref, ref, p_s.at[h, way, j - 1, i], p_r.at[h, way, j - 1, i], z_at(1 - 2 * way)).wait_recv()
+
+    def compute(h, j):
+        ways = [way for way in range(2) if j < sends(way, h)]
+        slots = [need_slot((sends(0, h) - j) % Z), need_slot((j - sends(1, h)) % Z)]
+        first = ways[0]
+
+        @pl.loop(0, 3 * len(ways))
+        def _(q):
+            way, i = first + q // 3, q % 3
+            part[way, i] = product((1 - way) * slots[0] + way * slots[1], h, i)
+
+    def forward(h, j):
+        ways = [way for way in range(2) if j < sends(way, h)]
+        first, count = ways[0], len(ways)
+
+        @pl.loop(0, 3 * count)
+        def _(q):
+            way, i = first + q % count, q // count
+            if j == 0:
+                ring[h, way, j, i] = coded(part[way, i])
+            else:
+                arrived(way, h, j, i)
+                ring[h, way, j, i] = coded(plain(ring[h, way, j, i]) + part[way, i])
+            hop(way, h, j, i).start()
+
+    def project(h):
+        @pl.loop(0, 3)
+        def _(i):
+            part[0, i] = product(Z - 1, h, i)
+
+    def settle(h):
+        @pl.loop(0, 3)
+        def _(i):
             for way in range(2):
-                go(w_copy(way, h, 0, p, 0))
-
-    own(0)
-    inject(0)
-    xg[core, c] = x_ref[...]
-    for d in range(1, S):
-        go(remote(xg.at[core, c], xg.at[core, c], xy_s.at[d - 1], xy_r.at[d - 1], y_at(d)))
-    own(1)
-
-    def x_second():
-        for d in range(1, S):
-            ref = xg.at[core, x * S + (y - d) % S]
-            remote(ref, ref, xy_s.at[d - 1], xy_r.at[d - 1], y_at(d)).wait_recv()
-        mine = xg.at[core, pl.ds(x * S, S)]
-        for d in range(1, S):
-            go(remote(mine, mine, xx_s.at[d - 1], xx_r.at[d - 1], x_at(d)))
-        go(remote(mine, mine, xc_s.at[0], xc_r.at[0], other))
-
-    def x_third():
-        for d in range(1, S):
-            ref = xg.at[core, pl.ds(((x - d) % S) * S, S)]
-            remote(ref, ref, xx_s.at[d - 1], xx_r.at[d - 1], x_at(d)).wait_recv()
-            go(remote(ref, ref, xc_s.at[d], xc_r.at[d], other))
-
-    def x_last():
-        for d in range(S):
-            ref = xg.at[1 - core, pl.ds(((x - d) % S) * S, S)]
-            remote(ref, ref, xc_s.at[d], xc_r.at[d], other).wait_recv()
-
-    def project(h):
-        acc[...] = jnp.zeros_like(acc)
-
-        @pl.loop(0, Z)
-        def _(s):
-            for i in range(3):
-                total = acc[i]
-                for p in range(2):
-                    total += jnp.dot(xg[p, s], wg[h, s, p, i], preferred_element_type=jnp.float32)
-                acc[i] = total
+                arrived(way, h, sends(way, h), i)
+            total = part[0, i] + plain(ring[h, 0, sends(0, h), i]) + plain(ring[h, 1, sends(1, h), i])
+            acc[i] = total * (1.0 / SCALE)
 
     def halo_copy(h):
         return remote(pad.at[h, :, pl.ds(TOK, 8)], halo.at[h], h_s.at[h], h_r.at[h], z_at(1))
 
     def part1(h):
         for i in range(3):
-            pad[h, i, 8:, :] = acc[i].astype(jnp.bfloat16).astype(jnp.float32)
+            pad[h, i, 8:, :] = acc[i]
         go(halo_copy(h))
 
     def lanes(h):
@@ -185,49 +272,64 @@
         gated = query[h] * (total + skip_ref[:, lanes(h)] * drive[h])
         out_ref[:, lanes(h)] = gated.astype(jnp.bfloat16)
 
-    for step in range(Z):
-        h, k = step // (Z // 2), step % (Z // 2) + 1
-        for p in range(2):
-            for way in range(2):
-                if valid(way, k, p):
-                    w_copy(way, h, k - 1, p, k).wait_recv()
-                    if k < Z // 2 and valid(way, k + 1, p):
-                        go(w_copy(way, h, k, p, k))
-        if h == 0 and k == Z // 2 - 1:
-            inject(1)
-        if step == 0:
-            x_second()
-        if step == 4:
-            x_third()
-        if step == 5:
-            x_last()
-        if step == 7:
-            project(0)
-            part1(0)
-        if step == 9:
+    for n in range(len(CHUNKS)):
+        x_first(n)
+    for n in range(len(CHUNKS)):
+        x_second(n)
+    ready = {first // 2: n for n, (first, count) in enumerate(CHUNKS)}
+    for j in range(Z // 2):
+        if j in ready:
+            x_third(ready[j])
+            x_last(ready[j])
+        compute(0, j)
+        forward(0, j)
+    compute(1, 0)
+    forward(1, 0)
+    project(0)
+    settle(0)
+    part1(0)
+    for j in range(1, Z // 2):
+        compute(1, j)
+        forward(1, j)
+        if j == 2:
             part2(0)
-        if step == 11:
+        if j == 4:
             part3(0)
     project(1)
+    settle(1)
     part1(1)
     part2(1)
     part3(1)
     for copy in started:
         copy.wait_send()
 
+    @pl.when(c != z)
+    def _():
+        scatter(0).wait_send()
+
+    for h in range(2):
+        for way in range(2):
+
+            @pl.loop(0, 3 * sends(way, h))
+            def _(q):
+                hop(way, h, q // 3, q % 3).wait_send()
+
 
 def per_device(inputs, w_in, short_filter, rates, residues, skip):
     vmem = pl.BlockSpec(memory_space=pltpu.VMEM)
     dma = pltpu.SemaphoreType.DMA
     f32, bf16 = jnp.float32, jnp.bfloat16
+    n = len(CHUNKS)
     return pl.pallas_call(
         kernel,
         out_shape=jax.ShapeDtypeStruct(inputs.shape, jnp.bfloat16),
         in_specs=[vmem] * 6,
         out_specs=vmem,
         scratch_shapes=[
-            pltpu.VMEM((2, Z, 2, 3, 256, LANE), bf16),
-            pltpu.VMEM((2, 16, TOK, 256), bf16),
+            pltpu.VMEM((TOK, 256), bf16),
+            pltpu.VMEM((2, Z, TOK, 256), bf16),
+            pltpu.VMEM((2, 2, Z // 2 + 1, 3, TOK, LANE), bf16),
+            pltpu.VMEM((2, 3, TOK, LANE), f32),
             pltpu.VMEM((3, TOK, LANE), f32),
             pltpu.VMEM((2, 3, TOK + 8, LANE), f32),
             pltpu.VMEM((2, 3, 8, LANE), f32),
@@ -235,8 +337,9 @@
             pltpu.VMEM((2, TOK, LANE), f32),
             pltpu.VMEM((2, Z, MODES, LANE), f32),
             pltpu.VMEM((TOK * 8, LANE), f32),
-            dma((3,)), dma((3,)), dma((3,)), dma((3,)), dma((4,)), dma((4,)),
-            dma((2, 2, 8, 2)), dma((2, 2, 8, 2)), dma((2,)), dma((2,)),
+            dma((Z,)), dma((Z,)),
+            dma((n, S - 1)), dma((n, S - 1)), dma((n, S - 1)), dma((n, S - 1)), dma((n, S)), dma((n, S)),
+            dma((2, 2, Z // 2, 3)), dma((2, 2, Z // 2, 3)), dma((2,)), dma((2,)),
             dma((2, Z - 1)), dma((2, Z - 1)),
         ],
         compiler_params=pltpu.CompilerParams(

time: 178 us -> 155 us (0.87)
  Pallas kernels: 172 us -> 149 us
    pallas_call x1, Pallas kernels: 172 us -> 149 us  [per_device(): pl.pallas_call(kernel, out_shape=jax.ShapeDtypeStruct(inputs.shape, jnp.b...]
where the time goes in v2:
time: 155 us
  Pallas kernels  149 us (96%)
  local copies, waits for them, and re-layouts  5.51 us (4%)
    pallas_call x1, Pallas kernels, per_device(): pl.pallas_call(kernel, out_shape=jax.ShapeDtypeStruct(inputs.shape, jnp.b...  149 us
    unnamed x13, local copies, waits for them, and re-layouts  5.51 us

profile of v2, /device:TPU:24, one launch (start us, length us, event | category | flops | bytes accessed | tf_op | source)
XLA Modules:
  0.0 154.7 jit_solution(14281362335180172752)
XLA Ops:
  0.0 0.0 copy-start.5
  0.0 0.7 copy-done.5
  0.7 0.0 copy-start
  0.7 1.1 copy-done
  1.8 0.0 copy-start.1
  1.8 0.9 copy-done.1
  2.7 0.0 copy-start.2
  2.7 0.7 copy-done.2
  3.4 0.0 copy-start.3
  3.4 0.7 copy-done.3
  4.2 0.0 copy-start.4
  4.2 0.7 copy-done.4
  4.9 149.1 %shard_map.64 = bf16[256,256]{1,0:T(8,128)(2,1)S(1)} custom-call(bf16[256,256]{1,0:T(8,128)(2,1)S(1)} %copy-done.1, bf16[3,512,256]{2,1,0:T(8,128)(2,1)S(1)} %copy-done, f32[3,3,256]{2,1,0:T(4,128)S(1)} %copy-done.4, f32[16,256]{1,0:T(8,128)S(1)} %copy-done.2, f32[16,256]{1,0:T(8,128)S(1)} %copy-done.3, f32[1,256]{1,0:T(1,128)S(1)} %bitcast.1), custom_call_target="tpu_custom_call" | custom-call | tf_op jit(solution)/shard_map/pallas_call | solution.py:323
  154.0 0.7 copy.8
Async XLA Ops:
  0.0 0.7 copy-start.5
  0.7 1.1 copy-start
  1.8 0.9 copy-start.1
  2.7 0.7 copy-start.2
  3.4 0.7 copy-start.3
  4.2 0.7 copy-start.4

commit v3 on v2

v3 whole, which is shorter than its diff:
```python
import functools

import jax
import jax.numpy as jnp
from jax import lax
from jax.experimental import pallas as pl
from jax.experimental.pallas import tpu as pltpu
from jax.sharding import PartitionSpec as P

MESH = pl.DeviceIdType.MESH
Z = 16
S = 4
TOK = 256
LANE = 128
MODES = 16
TAPS = 3


CHUNKS = ((0, 3), (3, 2), (5, 4), (9, 4), (13, 3))
SCALE = 2.0**16


def need_slot(tau):
    ahead = (tau - 1) % Z + 1
    late = (ahead - 1) // (Z // 2)
    return (1 - late) * (Z - 2 * ahead) + late * (2 * ahead - Z - 1)


def need_tau(r):
    return Z // 2 - r // 2 if r % 2 == 0 else (r + Z + 1) // 2


def coded(total):
    return (total * jnp.abs(total) * (total * total)).astype(jnp.bfloat16)


def plain(sent):
    fourth = sent.astype(jnp.float32)
    root = lax.rsqrt(jnp.maximum(jnp.abs(fourth), 1e-37))
    return fourth * root * root * lax.rsqrt(root)


def kernel(
    x_hbm, w_hbm, sf_hbm, rates_hbm, res_hbm, skip_hbm, out_ref,
    x_ref, w_ref, sf_ref, rates_ref, res_ref, skip_ref,
    xs, xp, xg, ring, part, acc, pad, halo, query, drive, est, states_in, ysum,
    in_s, p1_s, p1_r, p2_s, p2_r, xd_s, xd_r, xy_s, xy_r, xx_s, xx_r, xc_s, xc_r, p_s, p_r, h_s, h_r, e_s, e_r,
):
    loads = [
        pltpu.make_async_copy(a, b, in_s.at[n])
        for n, (a, b) in enumerate(
            [(x_hbm, x_ref), (w_hbm, w_ref), (sf_hbm, sf_ref), (rates_hbm, rates_ref), (res_hbm, res_ref), (skip_hbm, skip_ref)]
        )
    ]
    for load in loads:
        load.start()
    z = lax.axis_index("seq")
    ch = lax.axis_index("ch")
    core = ch % 2
    y = (ch // 2) % S
    x = ch // (2 * S)
    c = ch // 2

    def z_at(d):
        return ((z + d) % Z, ch)

    def c_at(d):
        return (z, ((c + d) % Z) * 2 + core)

    def y_at(d):
        return (z, (x * S + (y + d) % S) * 2 + core)

    def x_at(d):
        return (z, (((x + d) % S) * S + y) * 2 + core)

    other = (z, c * 2 + 1 - core)
    barrier = pltpu.get_barrier_semaphore()
    partners = [z_at(d) for d in range(1, Z)] + [c_at(d) for d in range(1, Z)] + [other]
    for p in partners:
        pl.semaphore_signal(barrier, inc=1, device_id=p, device_id_type=MESH)
    loads[0].wait()
    xs[...] = x_ref[...] * jnp.bfloat16(SCALE)
    pl.semaphore_wait(barrier, len(partners))

    started = []

    def remote(src, dst, ss, rs, dev):
        return pltpu.make_async_remote_copy(
            src_ref=src, dst_ref=dst, send_sem=ss, recv_sem=rs, device_id=dev, device_id_type=MESH
        )

    def go(copy):
        copy.start()
        started.append(copy)

    def rows16(at):
        return pl.ds(pl.multiple_of(at * 16, 16), 16)

    mine = rows16(c)

    for d in range(1, Z):
        go(remote(xs.at[rows16((c + d) % Z)], xp.at[c], p1_s.at[d - 1], p1_r.at[d - 1], c_at(d)))
    xp[c] = xs[mine]
    for d in range(1, Z):
        ref = xp.at[(c - d) % Z]
        remote(ref, ref, p1_s.at[d - 1], p1_r.at[d - 1], c_at(d)).wait_recv()
    for r in range(Z - 1):
        tau = need_tau(r)
        go(remote(xp.at[(z - tau) % Z], xg.at[core, r, mine], p2_s.at[r], p2_r.at[r], z_at(-tau)))
    xg[core, Z - 1, mine] = xp[z]

    def scattered(n):
        first, count = CHUNKS[n]
        for r in range(first, min(first + count, Z - 1)):
            ref = xg.at[core, r, mine]
            remote(ref, ref, p2_s.at[r], p2_r.at[r], other).wait_recv()

    def bundle(which, n, at, rows):
        first, count = CHUNKS[n]
        return xg.at[which, pl.ds(first, count), pl.ds(pl.multiple_of(at * rows, 16), rows)]

    def direct(n):
        scattered(n)
        ref = bundle(core, n, c, 16)
        for d in range(1, Z):
            go(remote(ref, ref, xd_s.at[d - 1], xd_r.at[d - 1], c_at(d)))

    def whole(which, n):
        return xg.at[which, pl.ds(*CHUNKS[n])]

    def direct_pass(n):
        for d in range(1, Z):
            ref = bundle(core, n, (c - d) % Z, 16)
            remote(ref, ref, xd_s.at[d - 1], xd_r.at[d - 1], c_at(d)).wait_recv()
        ref = whole(core, n)
        go(remote(ref, ref, xc_s.at[n, 0], xc_r.at[n, 0], other))

    def direct_last(n):
        ref = whole(1 - core, n)
        remote(ref, ref, xc_s.at[n, 0], xc_r.at[n, 0], other).wait_recv()

    def x_first(n):
        scattered(n)
        ref = bundle(core, n, c, 16)
        for d in range(1, S):
            go(remote(ref, ref, xy_s.at[n, d - 1], xy_r.at[n, d - 1], y_at(d)))

    def x_second(n):
        for d in range(1, S):
            ref = bundle(core, n, x * S + (y - d) % S, 16)
            remote(ref, ref, xy_s.at[n, d - 1], xy_r.at[n, d - 1], y_at(d)).wait_recv()
        ref = bundle(core, n, x, 64)
        for d in range(1, S):
            go(remote(ref, ref, xx_s.at[n, d - 1], xx_r.at[n, d - 1], x_at(d)))
        go(remote(ref, ref, xc_s.at[n, 0], xc_r.at[n, 0], other))

    def x_third(n):
        for d in range(1, S):
            ref = bundle(core, n, (x - d) % S, 64)
            remote(ref, ref, xx_s.at[n, d - 1], xx_r.at[n, d - 1], x_at(d)).wait_recv()
            go(remote(ref, ref, xc_s.at[n, d], xc_r.at[n, d], other))

    def x_last(n):
        for d in range(S):
            ref = bundle(1 - core, n, (x - d) % S, 64)
            remote(ref, ref, xc_s.at[n, d], xc_r.at[n, d], other).wait_recv()

    def lanes(h):
        return pl.ds(LANE * h, LANE)

    def long_way(h, i):
        return h + (1 - 2 * h) * (i // 2)

    def product(r, h, i):
        k = (i + 1) % 3
        total = jnp.dot(xg[0, r], w_ref[k, 0:256, lanes(h)], preferred_element_type=jnp.float32)
        return total + jnp.dot(xg[1, r], w_ref[k, 256:512, lanes(h)], preferred_element_type=jnp.float32)

    def hop(way, h, j, i):
        return remote(
            ring.at[h, way, j, i], ring.at[h, way, j + 1, i],
            p_s.at[h, way, j, i], p_r.at[h, way, j, i], z_at(1 - 2 * way),
        )

    def arrived(way, h, j, i):
        ref = ring.at[h, way, j, i]
        remote(ref, ref, p_s.at[h, way, j - 1, i], p_r.at[h, way, j - 1, i], z_at(1 - 2 * way)).wait_recv()

    def each(h, j, body):
        half = Z // 2
        last = j == half - 1

        @pl.loop(0, 3 if last else 6)
        def _(q):
            i = q if last else q // 2
            up = 1 - long_way(h, i)
            way = 1 - up if last else q % 2
            ups = up * need_slot(half - j) + (1 - up) * need_slot(half - 1 - j)
            downs = up * need_slot(half + 1 + j) + (1 - up) * need_slot(half + j)
            body(way, i, (1 - way) * ups + way * downs)

    def launch(h):
        def body(way, i, r):
            ring[h, way, 0, i] = coded(product(r, h, i))
            hop(way, h, 0, i).start()

        each(h, 0, body)

    def compute(h, j):
        def body(way, i, r):
            part[way, i] = product(r, h, i)

        each(h, j, body)

    def forward(h, j):
        def body(way, i, r):
            arrived(way, h, j, i)
            ring[h, way, j, i] = coded(plain(ring[h, way, j, i]) + part[way, i])
            hop(way, h, j, i).start()

        each(h, j, body)

    def project(h):
        @pl.loop(0, 3)
        def _(i):
            acc[i] = product(Z - 1, h, i)

    def settle(h, first, count):
        @pl.loop(first, first + count)
        def _(i):
            ends = [Z // 2 - long_way(h, i), Z // 2 - 1 + long_way(h, i)]
            for way in range(2):
                arrived(way, h, ends[way], i)
            total = acc[i] + plain(ring[h, 0, ends[0], i]) + plain(ring[h, 1, ends[1], i])
            pad[h, i, 8:, :] = total * (1.0 / SCALE)

    def halo_copy(h, n):
        which = pl.ds(0, 2) if n == 0 else pl.ds(2, 1)
        return remote(pad.at[h, which, pl.ds(TOK, 8)], halo.at[h, which], h_s.at[h, n], h_r.at[h, n], z_at(1))

    def part1(h):
        settle(h, 0, 2)
        go(halo_copy(h, 0))
        settle(h, 2, 1)
        go(halo_copy(h, 1))

    def state_copy(h, d, src, to):
        return remote(est.at[h, src], est.at[h, src], e_s.at[h, d - 1], e_r.at[h, d - 1], to)

    def mix(h, i):
        pad[h, i, 0:8, :] = halo[h, i] * (z > 0).astype(jnp.float32)
        total = jnp.zeros((TOK, LANE), jnp.float32)
        for j in range(TAPS):
            total += sf_ref[(i + 1) % 3, pl.ds(j, 1), lanes(h)] * pad[h, i, 8 - j : 8 - j + TOK, :]
        return total

    def part2(h):
        halo_copy(h, 0).wait_recv()
        drive[h] = mix(h, 0) * mix(h, 1)
        r = rates_ref[:, lanes(h)]
        f8 = jnp.exp(-8.0 * r)
        steps = [jnp.broadcast_to(f8[m : m + 1, :], (8, LANE)) for m in range(MODES)]

        def one(g, states):
            d = drive[h, pl.ds(pl.multiple_of(g * 8, 8), 8), :]
            return tuple(s * f + d for s, f in zip(states, steps))

        states = lax.fori_loop(0, TOK // 8, one, tuple(jnp.zeros((8, LANE), jnp.float32) for _ in range(MODES)))
        left = 7.0 - lax.broadcasted_iota(jnp.int32, (8, LANE), 0).astype(jnp.float32)
        for m in range(MODES):
            weight = jnp.exp(-r[m : m + 1, :] * left)
            states_in[pl.ds(m, 1), :] = jnp.sum(states[m] * weight, axis=0, keepdims=True)
        end = states_in[...]
        est[h, z] = (end * jnp.abs(end)).astype(jnp.bfloat16)
        for d in range(1, Z):
            go(state_copy(h, d, z, z_at(d)))
        halo_copy(h, 1).wait_recv()
        query[h] = mix(h, 2)

    def part3(h):
        for d in range(1, Z):
            state_copy(h, d, (z - d) % Z, z_at(d)).wait_recv()
        r = rates_ref[:, lanes(h)]
        block = jnp.exp(-float(TOK) * r)
        entering = jnp.zeros((MODES, LANE), jnp.float32)
        for s in range(Z - 1):
            square = est[h, s].astype(jnp.float32)
            end = square * lax.rsqrt(jnp.maximum(jnp.abs(square), 1e-37))
            entering = jnp.where(s < z, entering * block + end, entering)
        factor = jnp.exp(-r)
        scaled = res_ref[:, lanes(h)] * jnp.sqrt(1.0 - jnp.exp(-2.0 * r))
        fa, fb, sa, sb = factor[:8], factor[8:], scaled[:8], scaled[8:]

        def one(g, state):
            a, b = state
            base = pl.multiple_of(g * 8, 8)
            for t in range(8):
                d = drive[h, pl.ds(base + t, 1), :]
                a = a * fa + d
                b = b * fb + d
                ysum[pl.ds(pl.multiple_of((base + t) * 8, 8), 8), :] = a * sa + b * sb
            return a, b

        lax.fori_loop(0, TOK // 8, one, (entering[:8], entering[8:]))
        total = ysum[pl.ds(0, TOK, stride=8), :]
        for i in range(1, 8):
            total += ysum[pl.ds(i, TOK, stride=8), :]
        gated = query[h] * (total + skip_ref[:, lanes(h)] * drive[h])
        out_ref[:, lanes(h)] = gated.astype(jnp.bfloat16)

    direct(0)
    for load in loads[1:]:
        load.wait()
    x_first(1)
    direct_pass(0)
    for n in range(2, len(CHUNKS)):
        x_first(n)
    x_second(1)
    x_second(2)
    direct_last(0)
    launch(0)
    x_second(3)
    x_second(4)
    ready = {1: 1, 2: 2, 4: 3, 6: 4}
    for j in range(1, Z // 2):
        if j in ready:
            x_third(ready[j])
            x_last(ready[j])
        compute(0, j)
        forward(0, j)
    launch(1)
    project(0)
    part1(0)
    project(1)
    for j in range(1, Z // 2):
        compute(1, j)
        forward(1, j)
        if j == 2:
            part2(0)
        if j == 4:
            part3(0)
    part1(1)
    part2(1)
    part3(1)
    for copy in started:
        copy.wait_send()
    for h in range(2):
        for j in range(Z // 2):

            def drained(way, i, r):
                hop(way, h, j, i).wait_send()

            each(h, j, drained)


def per_device(inputs, w_in, short_filter, rates, residues, skip):
    dma = pltpu.SemaphoreType.DMA
    f32, bf16 = jnp.float32, jnp.bfloat16
    n = len(CHUNKS)
    args = (inputs, w_in, short_filter, rates, residues, skip.reshape(1, -1))
    return pl.pallas_call(
        kernel,
        out_shape=jax.ShapeDtypeStruct(inputs.shape, jnp.bfloat16),
        in_specs=[pl.BlockSpec(memory_space=pl.ANY)] * 6,
        out_specs=pl.BlockSpec(memory_space=pltpu.VMEM),
        scratch_shapes=[pltpu.VMEM(a.shape, a.dtype) for a in args]
        + [
            pltpu.VMEM((TOK, 256), bf16),
            pltpu.VMEM((Z, 16, 256), bf16),
            pltpu.VMEM((2, Z, TOK, 256), bf16),
            pltpu.VMEM((2, 2, Z // 2 + 1, 3, TOK, LANE), bf16),
            pltpu.VMEM((2, 3, TOK, LANE), f32),
            pltpu.VMEM((3, TOK, LANE), f32),
            pltpu.VMEM((2, 3, TOK + 8, LANE), f32),
            pltpu.VMEM((2, 3, 8, LANE), f32),
            pltpu.VMEM((2, TOK, LANE), f32),
            pltpu.VMEM((2, TOK, LANE), f32),
            pltpu.VMEM((2, Z, MODES, LANE), bf16),
            pltpu.VMEM((MODES, LANE), f32),
            pltpu.VMEM((TOK * 8, LANE), f32),
            dma((6,)),
            dma((Z - 1,)), dma((Z - 1,)), dma((Z - 1,)), dma((Z - 1,)), dma((Z - 1,)), dma((Z - 1,)),
            dma((n, S - 1)), dma((n, S - 1)), dma((n, S - 1)), dma((n, S - 1)), dma((n, S)), dma((n, S)),
            dma((2, 2, Z // 2, 3)), dma((2, 2, Z // 2, 3)), dma((2, 2)), dma((2, 2)),
            dma((2, Z - 1)), dma((2, Z - 1)),
        ],
        compiler_params=pltpu.CompilerParams(
            collective_id=0, has_side_effects=True, vmem_limit_bytes=60 * 2**20
        ),
    )(*args)


def solution(mesh):
    in_specs = (
        P("seq", "ch"),
        P(None, "seq", "ch"),
        P(None, None, "ch"),
        P(None, "ch"),
        P(None, "ch"),
        P("ch"),
    )
    return jax.shard_map(
        per_device, mesh=mesh, in_specs=in_specs, out_specs=P("seq", "ch"), check_vma=False
    )
```

time: 155 us -> 138 us (0.89); the launches traced: 155 us -> 135 us
  Pallas kernels: 149 us -> 134 us
  local copies, waits for them, and re-layouts: 5.51 us -> 1.57 us
    pallas_call x1, Pallas kernels: 149 us -> 134 us  [per_device(): pl.pallas_call(kernel, out_shape=jax.ShapeDtypeStruct(inputs.shape, jnp.b...]
    unnamed x13 -> x1, local copies, waits for them, and re-layouts: 5.51 us -> 1.57 us
where the time goes in v3:
time: 138 us; the launch traced here: 135 us
  Pallas kernels  134 us (97%)
  local copies, waits for them, and re-layouts  1.57 us (1%)
    pallas_call x1, Pallas kernels, per_device(): pl.pallas_call(kernel, out_shape=jax.ShapeDtypeStruct(inputs.shape, jnp.b...  134 us

profile of v3, /device:TPU:24, one launch (start us, length us, event | category | flops | bytes accessed | tf_op | source)
XLA Modules:
  0.0 135.3 jit_solution(13668583423464305358)
XLA Ops:
  0.0 133.7 %shard_map.64 = bf16[256,256]{1,0:T(8,128)(2,1)} custom-call(bf16[256,256]{1,0:T(8,128)(2,1)} %x_hbm.1, bf16[3,512,256]{2,1,0:T(8,128)(2,1)} %w_hbm.1, f32[3,3,256]{2,1,0:T(4,128)} %sf_hbm.1, f32[16,256]{1,0:T(8,128)} %rates_hbm.1, f32[16,256]{1,0:T(8,128)} %res_hbm.1, f32[1,256]{1,0:T(1,128)} %bitcast.1), custom_call_target="tpu_custom_call" | custom-call | tf_op jit(solution)/shard_map/pallas_call | solution.py:361
  133.7 1.6 %copy.8 = bf16[256,256]{1,0:T(8,128)(2,1)} copy(bf16[256,256]{1,0:T(8,128)(2,1)} %shard_map.64) | data formatting | bytes 262144

commit v4 on v3

v4 whole, which is shorter than its diff:
```python
import jax
import jax.numpy as jnp
from jax import lax
from jax.experimental import pallas as pl
from jax.experimental.pallas import tpu as pltpu
from jax.sharding import PartitionSpec as P

MESH = pl.DeviceIdType.MESH
Z = 16
HALF = Z // 2
S = 4
TOK = 256
EXT = TOK + 16
LANE = 128
MODES = 16
TAPS = 3
LAG = 5
CHUNKS = ((0, 3), (3, 2), (5, 4), (9, 4), (13, 3))
DIRECT = 2
QROWS = ((0, 144), (144, 128))
SCALE = 2.0**16


def need_slot(tau):
    ahead = (tau - 1) % Z + 1
    late = (ahead - 1) // HALF
    return (1 - late) * (Z - 2 * ahead) + late * (2 * ahead - Z - 1)


def need_tau(r):
    return HALF - r // 2 if r % 2 == 0 else (r + Z + 1) // 2


def coded(total):
    return (total * jnp.abs(total) * (total * total)).astype(jnp.bfloat16)


def plain(sent):
    fourth = sent.astype(jnp.float32)
    root = lax.rsqrt(jnp.maximum(jnp.abs(fourth), 1e-37))
    return fourth * root * root * lax.rsqrt(root)


def kernel(
    x_hbm, w_hbm, sf_hbm, rates_hbm, res_hbm, skip_hbm, out_ref,
    x_ref, w_ref, sf_ref, rates_ref, res_ref, skip_ref,
    xs, xp, xg, ring, qring, part, qpart, own, qown, pad, qpad, halo, drive, conv, est, ends, ysum,
    in_s, p1_s, p1_r, p2_s, p2_r, xd_s, xd_r, xy_s, xy_r, xx_s, xx_r, xc_s, xc_r,
    a_s, a_r, b_s, b_r, h_s, h_r, e_s, e_r,
):
    loads = [
        pltpu.make_async_copy(a, b, in_s.at[n])
        for n, (a, b) in enumerate(
            [(x_hbm, x_ref), (w_hbm, w_ref), (sf_hbm, sf_ref), (rates_hbm, rates_ref), (res_hbm, res_ref), (skip_hbm, skip_ref)]
        )
    ]
    for load in loads:
        load.start()
    z = lax.axis_index("seq")
    ch = lax.axis_index("ch")
    core = ch % 2
    y = (ch // 2) % S
    x = ch // (2 * S)
    c = ch // 2

    def z_at(d):
        return ((z + d) % Z, ch)

    def c_at(d):
        return (z, ((c + d) % Z) * 2 + core)

    def y_at(d):
        return (z, (x * S + (y + d) % S) * 2 + core)

    def x_at(d):
        return (z, (((x + d) % S) * S + y) * 2 + core)

    other = (z, c * 2 + 1 - core)
    barrier = pltpu.get_barrier_semaphore()
    partners = [z_at(d) for d in range(1, Z)] + [c_at(d) for d in range(1, Z)] + [other]
    for p in partners:
        pl.semaphore_signal(barrier, inc=1, device_id=p, device_id_type=MESH)
    loads[0].wait()
    xs[...] = x_ref[...] * jnp.bfloat16(SCALE)
    pl.semaphore_wait(barrier, len(partners))

    def remote(src, dst, ss, rs, dev):
        return pltpu.make_async_remote_copy(
            src_ref=src, dst_ref=dst, send_sem=ss, recv_sem=rs, device_id=dev, device_id_type=MESH
        )

    def take(ref, sem):
        pltpu.make_async_copy(ref, ref, sem).wait()

    def rows16(at):
        return pl.ds(pl.multiple_of(at * 16, 16), 16)

    mine = rows16(c)
    sent = []

    for d in range(1, Z):
        remote(xs.at[rows16((c + d) % Z)], xp.at[c], p1_s.at[0], p1_r.at[0], c_at(d)).start()
    xp[c] = xs[mine]
    take(xp.at[pl.ds(0, Z - 1)], p1_r.at[0])
    sent.append((xp.at[pl.ds(0, Z - 1)], p1_s.at[0]))

    def counted(n):
        first, count = CHUNKS[n]
        return first, min(first + count, Z - 1)

    def along(n):
        first, end = counted(n)
        for r in range(first, end):
            tau = need_tau(r)
            remote(xp.at[(z - tau) % Z], xg.at[core, r, mine], p2_s.at[n], p2_r.at[n], z_at(-tau)).start()
        sent.append((xp.at[pl.ds(0, end - first)], p2_s.at[n]))

    def scattered(n):
        first, end = counted(n)
        take(xg.at[core, pl.ds(first, end - first), mine], p2_r.at[n])

    def bundle(which, n, at, rows):
        first, count = CHUNKS[n]
        return xg.at[which, pl.ds(first, count), pl.ds(pl.multiple_of(at * rows, 16), rows)]

    def whole(which, n):
        return xg.at[which, pl.ds(*CHUNKS[n])]

    def part_of(n, rows):
        first, count = CHUNKS[n]
        return xg.at[core, pl.ds(first, count), pl.ds(0, rows)]

    def cross(n):
        ref = whole(core, n)
        remote(ref, ref, xc_s.at[n], xc_r.at[n], other).start()
        sent.append((ref, xc_s.at[n]))

    def crossed(n):
        take(whole(1 - core, n), xc_r.at[n])

    def direct(n):
        scattered(n)
        ref = bundle(core, n, c, 16)
        for d in range(1, Z):
            remote(ref, ref, xd_s.at[n], xd_r.at[n], c_at(d)).start()
        sent.append((part_of(n, 16 * (Z - 1)), xd_s.at[n]))

    def direct_pass(n):
        take(part_of(n, 16 * (Z - 1)), xd_r.at[n])
        cross(n)

    def x_first(n):
        scattered(n)
        ref = bundle(core, n, c, 16)
        for d in range(1, S):
            remote(ref, ref, xy_s.at[n - DIRECT], xy_r.at[n - DIRECT], y_at(d)).start()
        sent.append((part_of(n, 16 * (S - 1)), xy_s.at[n - DIRECT]))

    def x_second(n):
        take(part_of(n, 16 * (S - 1)), xy_r.at[n - DIRECT])
        ref = bundle(core, n, x, 64)
        for d in range(1, S):
            remote(ref, ref, xx_s.at[n - DIRECT], xx_r.at[n - DIRECT], x_at(d)).start()
        sent.append((part_of(n, 64 * (S - 1)), xx_s.at[n - DIRECT]))

    def x_third(n):
        take(part_of(n, 64 * (S - 1)), xx_r.at[n - DIRECT])
        cross(n)

    def lanes(h):
        return pl.ds(pl.multiple_of(LANE * h, LANE), LANE)

    def times(h, k, rows, r):
        total = jnp.dot(xg[0, r, rows], w_ref[k, 0:256, lanes(h)], preferred_element_type=jnp.float32)
        return total + jnp.dot(xg[1, r, rows], w_ref[k, 256:512, lanes(h)], preferred_element_type=jnp.float32)

    every, tail = slice(0, TOK), slice(TOK - 16, TOK)

    def chains(j, inner, body):
        last = j == HALF - 1

        @pl.loop(0, (2 if last else 4) * inner)
        def _(q):
            if last:
                h, i = q % 2, q // 2
                way = h
            else:
                way, h, i = q % 2, (q // 2) % 2, q // 4

            def pick(back):
                ups = (1 - h) * need_slot(HALF - j - back) + h * need_slot(HALF - 1 - j - back)
                downs = (1 - h) * need_slot(HALF + 1 + j - back) + h * need_slot(HALF + j - back)
                return (1 - way) * ups + way * downs

            body(way, h, i, pick)

    def a_hop(way, h, j, i):
        return remote(
            ring.at[h, way, j, i], ring.at[h, way, j + 1, i],
            a_s.at[h, way, i], a_r.at[h, way, j, i], z_at(1 - 2 * way),
        )

    def b_hop(way, h, j, p):
        rows = pl.ds(*QROWS[p])
        return remote(
            qring.at[h, way, j, rows], qring.at[h, way, j + 1, rows],
            b_s.at[h, way, p], b_r.at[h, way, j, p], z_at(1 - 2 * way),
        )

    def a_launch():
        def body(way, h, i, pick):
            ring[h, way, 0, i] = coded(times(h, i + 1, every, pick(0)))
            a_hop(way, h, 0, i).start()

        chains(0, 2, body)

    def a_compute(j):
        def body(way, h, i, pick):
            part[h, way, i] = times(h, i + 1, every, pick(0))

        chains(j, 2, body)

    def a_forward(j):
        def body(way, h, i, pick):
            a_hop(way, h, j - 1, i).wait()
            ring[h, way, j, i] = coded(plain(ring[h, way, j, i]) + part[h, way, i])
            a_hop(way, h, j, i).start()

        chains(j, 2, body)

    def b_compute(j):
        def body(way, h, i, pick):
            qpart[h, way, 0:16] = times(h, 0, tail, pick(1))
            qpart[h, way, 16:EXT] = times(h, 0, every, pick(0))

        chains(j, 1, body)

    def b_forward(j):
        def body(way, h, i, pick):
            for p in range(2):
                rows = slice(QROWS[p][0], sum(QROWS[p]))
                if j == 0:
                    qring[h, way, j, rows] = coded(qpart[h, way, rows])
                else:
                    b_hop(way, h, j - 1, p).wait()
                    qring[h, way, j, rows] = coded(plain(qring[h, way, j, rows]) + qpart[h, way, rows])
                b_hop(way, h, j, p).start()

        chains(j, 1, body)

    def a_own():
        @pl.loop(0, 4)
        def _(q):
            own[q // 2, q % 2] = times(q // 2, q % 2 + 1, every, Z - 1)

    def b_own():
        @pl.loop(0, 2)
        def _(h):
            qown[h, 0:16] = times(h, 0, tail, need_slot(-1))
            qown[h, 16:EXT] = times(h, 0, every, Z - 1)

    def halo_copy():
        return remote(pad.at[:, :, pl.ds(TOK, 8)], halo, h_s.at[0], h_r.at[0], z_at(1))

    def a_settle():
        @pl.loop(0, 4)
        def _(q):
            h, i = q // 2, q % 2
            stops = (HALF - h, HALF - 1 + h)
            for way in range(2):
                a_hop(way, h, stops[way] - 1, i).wait()
            total = own[h, i] + plain(ring[h, 0, stops[0], i]) + plain(ring[h, 1, stops[1], i])
            pad[h, i, 8:, :] = total * (1.0 / SCALE)

        halo_copy().start()

    first = (z > 0).astype(jnp.float32)

    def part2(h):
        mixed = []
        for i in range(2):
            pad[h, i, 0:8, :] = halo[h, i] * first
            total = jnp.zeros((TOK, LANE), jnp.float32)
            for j in range(TAPS):
                total += sf_ref[i + 1, pl.ds(j, 1), lanes(h)] * pad[h, i, 8 - j : 8 - j + TOK, :]
            mixed.append(total)
        drive[h] = mixed[0] * mixed[1]
        r = rates_ref[:, lanes(h)]
        f8 = jnp.exp(-8.0 * r)
        steps = [jnp.broadcast_to(f8[m : m + 1, :], (8, LANE)) for m in range(MODES)]

        def one(g, states):
            d = drive[h, pl.ds(pl.multiple_of(g * 8, 8), 8), :]
            return tuple(s * f + d for s, f in zip(states, steps))

        states = lax.fori_loop(0, TOK // 8, one, tuple(jnp.zeros((8, LANE), jnp.float32) for _ in range(MODES)))
        left = 7.0 - lax.broadcasted_iota(jnp.int32, (8, LANE), 0).astype(jnp.float32)
        for m in range(MODES):
            weight = jnp.exp(-r[m : m + 1, :] * left)
            ends[pl.ds(m, 1), :] = jnp.sum(states[m] * weight, axis=0, keepdims=True)
        end = ends[...]
        est[z, h] = (end * jnp.abs(end)).astype(jnp.bfloat16)

    def states_out():
        for d in range(1, Z):
            remote(est.at[z], est.at[z], e_s.at[0], e_r.at[0], z_at(d)).start()
        sent.append((est.at[pl.ds(0, Z - 1)], e_s.at[0]))

    def part3(h):
        r = rates_ref[:, lanes(h)]
        block = jnp.exp(-float(TOK) * r)
        entering = jnp.zeros((MODES, LANE), jnp.float32)
        for s in range(Z - 1):
            square = est[s, h].astype(jnp.float32)
            end = square * lax.rsqrt(jnp.maximum(jnp.abs(square), 1e-37))
            entering = jnp.where(s < z, entering * block + end, entering)
        factor = jnp.exp(-r)
        scaled = res_ref[:, lanes(h)] * jnp.sqrt(1.0 - jnp.exp(-2.0 * r))
        fa, fb, sa, sb = factor[:8], factor[8:], scaled[:8], scaled[8:]

        def one(g, state):
            a, b = state
            base = pl.multiple_of(g * 8, 8)
            for t in range(8):
                d = drive[h, pl.ds(base + t, 1), :]
                a = a * fa + d
                b = b * fb + d
                ysum[pl.ds(pl.multiple_of((base + t) * 8, 8), 8), :] = a * sa + b * sb
            return a, b

        lax.fori_loop(0, TOK // 8, one, (entering[:8], entering[8:]))
        total = ysum[pl.ds(0, TOK, stride=8), :]
        for i in range(1, 8):
            total += ysum[pl.ds(i, TOK, stride=8), :]
        conv[h] = total + skip_ref[:, lanes(h)] * drive[h]

    def finish(h):
        stops = (HALF - h, HALF - 1 + h)
        for p in range(2):
            for way in range(2):
                b_hop(way, h, stops[way] - 1, p).wait()
            rows = slice(QROWS[p][0], sum(QROWS[p]))
            total = qown[h, rows] + plain(qring[h, 0, stops[0], rows]) + plain(qring[h, 1, stops[1], rows])
            qpad[rows] = total * (1.0 / SCALE)
        qpad[0:16] = qpad[0:16] * first
        query = jnp.zeros((TOK, LANE), jnp.float32)
        for j in range(TAPS):
            query += sf_ref[0, pl.ds(j, 1), lanes(h)] * qpad[16 - j : 16 - j + TOK, :]
        out_ref[:, LANE * h : LANE * (h + 1)] = (query * conv[h]).astype(jnp.bfloat16)

    along(0)
    direct(0)
    for n in range(1, len(CHUNKS)):
        along(n)
    xg[core, Z - 1, mine] = xp[z]
    direct(1)
    for load in loads[1:]:
        load.wait()
    direct_pass(0)
    for n in range(DIRECT, len(CHUNKS)):
        x_first(n)
    direct_pass(1)
    crossed(0)
    a_launch()
    for n in range(DIRECT, len(CHUNKS)):
        x_second(n)
    ready = {1: 1, 2: 2, 4: 3, 6: 4}
    for step in range(1, HALF + LAG + 1):
        if step in ready:
            n = ready[step]
            if n >= DIRECT:
                x_third(n)
            crossed(n)
        if step < HALF:
            a_compute(step)
            a_forward(step)
        if step == HALF:
            a_settle()
        if LAG <= step < HALF + LAG:
            b_compute(step - LAG)
            b_forward(step - LAG)
        if step == HALF - 1:
            a_own()
        if step == HALF + 1:
            halo_copy().wait()
            part2(0)
            part2(1)
            states_out()
        if step == HALF + 2:
            b_own()
        if step == HALF + 3:
            take(est.at[pl.ds(0, Z - 1)], e_r.at[0])
            part3(0)
        if step == HALF + 4:
            part3(1)
    finish(0)
    finish(1)
    for ref, sem in sent:
        take(ref, sem)


def per_device(inputs, w_in, short_filter, rates, residues, skip):
    dma = pltpu.SemaphoreType.DMA
    f32, bf16 = jnp.float32, jnp.bfloat16
    n = len(CHUNKS)
    args = (inputs, w_in, short_filter, rates, residues, skip.reshape(1, -1))
    return pl.pallas_call(
        kernel,
        out_shape=jax.ShapeDtypeStruct(inputs.shape, jnp.bfloat16),
        in_specs=[pl.BlockSpec(memory_space=pl.ANY)] * 6,
        out_specs=pl.BlockSpec(memory_space=pltpu.VMEM),
        scratch_shapes=[pltpu.VMEM(a.shape, a.dtype) for a in args]
        + [
            pltpu.VMEM((TOK, 256), bf16),
            pltpu.VMEM((Z, 16, 256), bf16),
            pltpu.VMEM((2, Z, TOK, 256), bf16),
            pltpu.VMEM((2, 2, HALF + 1, 2, TOK, LANE), bf16),
            pltpu.VMEM((2, 2, HALF + 1, EXT, LANE), bf16),
            pltpu.VMEM((2, 2, 2, TOK, LANE), f32),
            pltpu.VMEM((2, 2, EXT, LANE), f32),
            pltpu.VMEM((2, 2, TOK, LANE), f32),
            pltpu.VMEM((2, EXT, LANE), f32),
            pltpu.VMEM((2, 2, TOK + 8, LANE), f32),
            pltpu.VMEM((EXT, LANE), f32),
            pltpu.VMEM((2, 2, 8, LANE), f32),
            pltpu.VMEM((2, TOK, LANE), f32),
            pltpu.VMEM((2, TOK, LANE), f32),
            pltpu.VMEM((Z, 2, MODES, LANE), bf16),
            pltpu.VMEM((MODES, LANE), f32),
            pltpu.VMEM((TOK * 8, LANE), f32),
            dma((6,)), dma((1,)), dma((1,)), dma((n,)), dma((n,)), dma((DIRECT,)), dma((DIRECT,)),
            dma((n - DIRECT,)), dma((n - DIRECT,)), dma((n - DIRECT,)), dma((n - DIRECT,)), dma((n,)), dma((n,)),
            dma((2, 2, 2)), dma((2, 2, HALF, 2)), dma((2, 2, 2)), dma((2, 2, HALF, 2)),
            dma((1,)), dma((1,)), dma((1,)), dma((1,)),
        ],
        compiler_params=pltpu.CompilerParams(
            collective_id=0, has_side_effects=True, vmem_limit_bytes=60 * 2**20
        ),
    )(*args)


def solution(mesh):
    in_specs = (
        P("seq", "ch"),
        P(None, "seq", "ch"),
        P(None, None, "ch"),
        P(None, "ch"),
        P(None, "ch"),
        P("ch"),
    )
    return jax.shard_map(
        per_device, mesh=mesh, in_specs=in_specs, out_specs=P("seq", "ch"), check_vma=False
    )
```

time: 138 us -> 124 us (0.90)
  Pallas kernels: 134 us -> 121 us
    pallas_call x1, Pallas kernels: 134 us -> 121 us  [per_device(): pl.pallas_call(kernel, out_shape=jax.ShapeDtypeStruct(inputs.shape, jnp.b...]
where the time goes in v4:
time: 124 us; the launch traced here: 123 us
  Pallas kernels  121 us (98%)
  local copies, waits for them, and re-layouts  1.57 us (1%)
    pallas_call x1, Pallas kernels, per_device(): pl.pallas_call(kernel, out_shape=jax.ShapeDtypeStruct(inputs.shape, jnp.b...  121 us

profile of v4, /device:TPU:24, one launch (start us, length us, event | category | flops | bytes accessed | tf_op | source)
XLA Modules:
  0.0 122.7 jit_solution(11636708454164203853)
XLA Ops:
  0.0 121.1 %shard_map.64 = bf16[256,256]{1,0:T(8,128)(2,1)} custom-call(bf16[256,256]{1,0:T(8,128)(2,1)} %x_hbm.1, bf16[3,512,256]{2,1,0:T(8,128)(2,1)} %w_hbm.1, f32[3,3,256]{2,1,0:T(4,128)} %sf_hbm.1, f32[16,256]{1,0:T(8,128)} %rates_hbm.1, f32[16,256]{1,0:T(8,128)} %res_hbm.1, f32[1,256]{1,0:T(1,128)} %bitcast.1), custom_call_target="tpu_custom_call" | custom-call | tf_op jit(solution)/shard_map/pallas_call | solution.py:407
  121.1 1.6 %copy.8 = bf16[256,256]{1,0:T(8,128)(2,1)} copy(bf16[256,256]{1,0:T(8,128)(2,1)} %shard_map.64) | data formatting | bytes 262144

commit v5 on v4

--- a/solution.py
+++ b/solution.py
@@ -14,11 +14,21 @@
 LANE = 128
 MODES = 16
 TAPS = 3
-LAG = 5
-CHUNKS = ((0, 3), (3, 2), (5, 4), (9, 4), (13, 3))
-DIRECT = 2
+LAG = 4
+CHUNKS = ((0, 1), (1, 2), (3, 2), (5, 2), (7, 2), (9, 4), (13, 3))
 QROWS = ((0, 144), (144, 128))
 SCALE = 2.0**16
+
+
+def hops(d, size):
+    return min(d % size, -d % size)
+
+
+PLANE = sorted(
+    [(i, j) for i in range(S) for j in range(S) if (i, j) != (0, 0)],
+    key=lambda d: -hops(d[0], S) - hops(d[1], S),
+)
+RING = sorted(range(1, Z), key=lambda d: -hops(d, Z))
 
 
 def need_slot(tau):
@@ -45,7 +55,7 @@
     x_hbm, w_hbm, sf_hbm, rates_hbm, res_hbm, skip_hbm, out_ref,
     x_ref, w_ref, sf_ref, rates_ref, res_ref, skip_ref,
     xs, xp, xg, ring, qring, part, qpart, own, qown, pad, qpad, halo, drive, conv, est, ends, ysum,
-    in_s, p1_s, p1_r, p2_s, p2_r, xd_s, xd_r, xy_s, xy_r, xx_s, xx_r, xc_s, xc_r,
+    in_s, p1_s, p1_r, p2_s, p2_r, xd_s, xd_r, xc_s, xc_r,
     a_s, a_r, b_s, b_r, h_s, h_r, e_s, e_r,
 ):
     loads = [
@@ -66,18 +76,15 @@
     def z_at(d):
         return ((z + d) % Z, ch)
 
+    def chip(d):
+        return ((x + d[0]) % S) * S + (y + d[1]) % S
+
     def c_at(d):
-        return (z, ((c + d) % Z) * 2 + core)
-
-    def y_at(d):
-        return (z, (x * S + (y + d) % S) * 2 + core)
-
-    def x_at(d):
-        return (z, (((x + d) % S) * S + y) * 2 + core)
+        return (z, chip(d) * 2 + core)
 
     other = (z, c * 2 + 1 - core)
     barrier = pltpu.get_barrier_semaphore()
-    partners = [z_at(d) for d in range(1, Z)] + [c_at(d) for d in range(1, Z)] + [other]
+    partners = [z_at(d) for d in RING] + [c_at(d) for d in PLANE] + [other]
     for p in partners:
         pl.semaphore_signal(barrier, inc=1, device_id=p, device_id_type=MESH)
     loads[0].wait()
@@ -98,8 +105,8 @@
     mine = rows16(c)
     sent = []
 
-    for d in range(1, Z):
-        remote(xs.at[rows16((c + d) % Z)], xp.at[c], p1_s.at[0], p1_r.at[0], c_at(d)).start()
+    for d in PLANE:
+        remote(xs.at[rows16(chip(d))], xp.at[c], p1_s.at[0], p1_r.at[0], c_at(d)).start()
     xp[c] = xs[mine]
     take(xp.at[pl.ds(0, Z - 1)], p1_r.at[0])
     sent.append((xp.at[pl.ds(0, Z - 1)], p1_s.at[0]))
@@ -141,30 +148,12 @@
     def direct(n):
         scattered(n)
         ref = bundle(core, n, c, 16)
-        for d in range(1, Z):
+        for d in PLANE:
             remote(ref, ref, xd_s.at[n], xd_r.at[n], c_at(d)).start()
         sent.append((part_of(n, 16 * (Z - 1)), xd_s.at[n]))
 
     def direct_pass(n):
         take(part_of(n, 16 * (Z - 1)), xd_r.at[n])
-        cross(n)
-
-    def x_first(n):
-        scattered(n)
-        ref = bundle(core, n, c, 16)
-        for d in range(1, S):
-            remote(ref, ref, xy_s.at[n - DIRECT], xy_r.at[n - DIRECT], y_at(d)).start()
-        sent.append((part_of(n, 16 * (S - 1)), xy_s.at[n - DIRECT]))
-
-    def x_second(n):
-        take(part_of(n, 16 * (S - 1)), xy_r.at[n - DIRECT])
-        ref = bundle(core, n, x, 64)
-        for d in range(1, S):
-            remote(ref, ref, xx_s.at[n - DIRECT], xx_r.at[n - DIRECT], x_at(d)).start()
-        sent.append((part_of(n, 64 * (S - 1)), xx_s.at[n - DIRECT]))
-
-    def x_third(n):
-        take(part_of(n, 64 * (S - 1)), xx_r.at[n - DIRECT])
         cross(n)
 
     def lanes(h):
@@ -207,12 +196,13 @@
             b_s.at[h, way, p], b_r.at[h, way, j, p], z_at(1 - 2 * way),
         )
 
-    def a_launch():
-        def body(way, h, i, pick):
-            ring[h, way, 0, i] = coded(times(h, i + 1, every, pick(0)))
-            a_hop(way, h, 0, i).start()
-
-        chains(0, 2, body)
+    def a_launch(starts, r):
+        for way, h in starts:
+
+            @pl.loop(0, 2)
+            def _(i):
+                ring[h, way, 0, i] = coded(times(h, i + 1, every, r))
+                a_hop(way, h, 0, i).start()
 
     def a_compute(j):
         def body(way, h, i, pick):
@@ -302,7 +292,7 @@
         est[z, h] = (end * jnp.abs(end)).astype(jnp.bfloat16)
 
     def states_out():
-        for d in range(1, Z):
+        for d in RING:
             remote(est.at[z], est.at[z], e_s.at[0], e_r.at[0], z_at(d)).start()
         sent.append((est.at[pl.ds(0, Z - 1)], e_s.at[0]))
 
@@ -349,31 +339,39 @@
         out_ref[:, LANE * h : LANE * (h + 1)] = (query * conv[h]).astype(jnp.bfloat16)
 
     along(0)
+    along(1)
+    along(2)
     direct(0)
-    for n in range(1, len(CHUNKS)):
-        along(n)
+    direct(1)
+    along(3)
+    along(4)
+    along(5)
+    along(6)
     xg[core, Z - 1, mine] = xp[z]
-    direct(1)
     for load in loads[1:]:
         load.wait()
+    direct(2)
     direct_pass(0)
-    for n in range(DIRECT, len(CHUNKS)):
-        x_first(n)
     direct_pass(1)
     crossed(0)
-    a_launch()
-    for n in range(DIRECT, len(CHUNKS)):
-        x_second(n)
-    ready = {1: 1, 2: 2, 4: 3, 6: 4}
+    a_launch(((0, 0), (1, 1)), need_slot(HALF))
+    direct(3)
+    crossed(1)
+    a_launch(((1, 0),), need_slot(HALF + 1))
+    a_launch(((0, 1),), need_slot(HALF - 1))
+    direct(4)
+    direct_pass(2)
+    direct(5)
+    direct(6)
+    ready = {1: 2, 2: 3, 3: 4, 4: 5, 6: 6}
     for step in range(1, HALF + LAG + 1):
         if step in ready:
-            n = ready[step]
-            if n >= DIRECT:
-                x_third(n)
-            crossed(n)
+            crossed(ready[step])
         if step < HALF:
             a_compute(step)
             a_forward(step)
+        if step + 1 in ready:
+            direct_pass(ready[step + 1])
         if step == HALF:
             a_settle()
         if LAG <= step < HALF + LAG:
@@ -428,8 +426,8 @@
             pltpu.VMEM((Z, 2, MODES, LANE), bf16),
             pltpu.VMEM((MODES, LANE), f32),
             pltpu.VMEM((TOK * 8, LANE), f32),
-            dma((6,)), dma((1,)), dma((1,)), dma((n,)), dma((n,)), dma((DIRECT,)), dma((DIRECT,)),
-            dma((n - DIRECT,)), dma((n - DIRECT,)), dma((n - DIRECT,)), dma((n - DIRECT,)), dma((n,)), dma((n,)),
+            dma((6,)), dma((1,)), dma((1,)), dma((n,)), dma((n,)), dma((n,)), dma((n,)),
+            dma((n,)), dma((n,)),
             dma((2, 2, 2)), dma((2, 2, HALF, 2)), dma((2, 2, 2)), dma((2, 2, HALF, 2)),
             dma((1,)), dma((1,)), dma((1,)), dma((1,)),
         ],

time: 124 us -> 115 us (0.927)
  Pallas kernels: 121 us -> 113 us
    pallas_call x1, Pallas kernels: 121 us -> 113 us  [per_device(): pl.pallas_call(kernel, out_shape=jax.ShapeDtypeStruct(inputs.shape, jnp.b...]
where the time goes in v5:
time: 115 us
  Pallas kernels  113 us (98%)
  local copies, waits for them, and re-layouts  1.57 us (1%)
    pallas_call x1, Pallas kernels, per_device(): pl.pallas_call(kernel, out_shape=jax.ShapeDtypeStruct(inputs.shape, jnp.b...  113 us

profile of v5, /device:TPU:24, one launch (start us, length us, event | category | flops | bytes accessed | tf_op | source)
XLA Modules:
  0.0 114.8 jit_solution(4152754165334621665)
XLA Ops:
  0.0 113.2 %shard_map.64 = bf16[256,256]{1,0:T(8,128)(2,1)} custom-call(bf16[256,256]{1,0:T(8,128)(2,1)} %x_hbm.1, bf16[3,512,256]{2,1,0:T(8,128)(2,1)} %w_hbm.1, f32[3,3,256]{2,1,0:T(4,128)} %sf_hbm.1, f32[16,256]{1,0:T(8,128)} %rates_hbm.1, f32[16,256]{1,0:T(8,128)} %res_hbm.1, f32[1,256]{1,0:T(1,128)} %bitcast.1), custom_call_target="tpu_custom_call" | custom-call | tf_op jit(solution)/shard_map/pallas_call | solution.py:405
  113.2 1.6 %copy.8 = bf16[256,256]{1,0:T(8,128)(2,1)} copy(bf16[256,256]{1,0:T(8,128)(2,1)} %shard_map.64) | data formatting | bytes 262144

commit v6 on v5

--- a/solution.py
+++ b/solution.py
@@ -14,7 +14,7 @@
 LANE = 128
 MODES = 16
 TAPS = 3
-LAG = 4
+LAG = 3
 CHUNKS = ((0, 1), (1, 2), (3, 2), (5, 2), (7, 2), (9, 4), (13, 3))
 QROWS = ((0, 144), (144, 128))
 SCALE = 2.0**16
@@ -379,17 +379,17 @@
             b_forward(step - LAG)
         if step == HALF - 1:
             a_own()
-        if step == HALF + 1:
+        if step == HALF:
             halo_copy().wait()
             part2(0)
             part2(1)
             states_out()
+        if step == HALF + 1:
+            b_own()
         if step == HALF + 2:
-            b_own()
-        if step == HALF + 3:
             take(est.at[pl.ds(0, Z - 1)], e_r.at[0])
             part3(0)
-        if step == HALF + 4:
+        if step == HALF + 3:
             part3(1)
     finish(0)
     finish(1)

time: 115 us -> 114 us (level); the launches traced: 115 us -> 112 us
  Pallas kernels: 113 us -> 111 us
    pallas_call x1, Pallas kernels: 113 us -> 111 us  [per_device(): pl.pallas_call(kernel, out_shape=jax.ShapeDtypeStruct(inputs.shape, jnp.b...]
where the time goes in v6:
time: 114 us; the launch traced here: 112 us
  Pallas kernels  111 us (97%)
  local copies, waits for them, and re-layouts  1.57 us (1%)
    pallas_call x1, Pallas kernels, per_device(): pl.pallas_call(kernel, out_shape=jax.ShapeDtypeStruct(inputs.shape, jnp.b...  111 us

profile of v6, /device:TPU:24, one launch (start us, length us, event | category | flops | bytes accessed | tf_op | source)
XLA Modules:
  0.0 112.3 jit_solution(9411287016948212012)
XLA Ops:
  0.0 110.8 %shard_map.64 = bf16[256,256]{1,0:T(8,128)(2,1)} custom-call(bf16[256,256]{1,0:T(8,128)(2,1)} %x_hbm.1, bf16[3,512,256]{2,1,0:T(8,128)(2,1)} %w_hbm.1, f32[3,3,256]{2,1,0:T(4,128)} %sf_hbm.1, f32[16,256]{1,0:T(8,128)} %rates_hbm.1, f32[16,256]{1,0:T(8,128)} %res_hbm.1, f32[1,256]{1,0:T(1,128)} %bitcast.1), custom_call_target="tpu_custom_call" | custom-call | tf_op jit(solution)/shard_map/pallas_call | solution.py:405
  110.8 1.6 %copy.8 = bf16[256,256]{1,0:T(8,128)(2,1)} copy(bf16[256,256]{1,0:T(8,128)(2,1)} %shard_map.64) | data formatting | bytes 262144

commit v7 on v6

--- a/solution.py
+++ b/solution.py
@@ -296,33 +296,39 @@
             remote(est.at[z], est.at[z], e_s.at[0], e_r.at[0], z_at(d)).start()
         sent.append((est.at[pl.ds(0, Z - 1)], e_s.at[0]))
 
-    def part3(h):
-        r = rates_ref[:, lanes(h)]
-        block = jnp.exp(-float(TOK) * r)
-        entering = jnp.zeros((MODES, LANE), jnp.float32)
-        for s in range(Z - 1):
-            square = est[s, h].astype(jnp.float32)
-            end = square * lax.rsqrt(jnp.maximum(jnp.abs(square), 1e-37))
-            entering = jnp.where(s < z, entering * block + end, entering)
-        factor = jnp.exp(-r)
-        scaled = res_ref[:, lanes(h)] * jnp.sqrt(1.0 - jnp.exp(-2.0 * r))
-        fa, fb, sa, sb = factor[:8], factor[8:], scaled[:8], scaled[8:]
-
-        def one(g, state):
-            a, b = state
+    def part3():
+        starts, gains = [], []
+        for h in range(2):
+            r = rates_ref[:, lanes(h)]
+            block = jnp.exp(-float(TOK) * r)
+            entering = jnp.zeros((MODES, LANE), jnp.float32)
+            for s in range(Z - 1):
+                square = est[s, h].astype(jnp.float32)
+                end = square * lax.rsqrt(jnp.maximum(jnp.abs(square), 1e-37))
+                entering = jnp.where(s < z, entering * block + end, entering)
+            factor = jnp.exp(-r)
+            scaled = res_ref[:, lanes(h)] * jnp.sqrt(1.0 - jnp.exp(-2.0 * r))
+            starts += [entering[:8], entering[8:]]
+            gains.append((factor[:8], factor[8:], scaled[:8], scaled[8:]))
+
+        def one(g, states):
+            states = list(states)
             base = pl.multiple_of(g * 8, 8)
             for t in range(8):
-                d = drive[h, pl.ds(base + t, 1), :]
-                a = a * fa + d
-                b = b * fb + d
-                ysum[pl.ds(pl.multiple_of((base + t) * 8, 8), 8), :] = a * sa + b * sb
-            return a, b
-
-        lax.fori_loop(0, TOK // 8, one, (entering[:8], entering[8:]))
-        total = ysum[pl.ds(0, TOK, stride=8), :]
-        for i in range(1, 8):
-            total += ysum[pl.ds(i, TOK, stride=8), :]
-        conv[h] = total + skip_ref[:, lanes(h)] * drive[h]
+                for h, (fa, fb, sa, sb) in enumerate(gains):
+                    d = drive[h, pl.ds(base + t, 1), :]
+                    a = states[2 * h] * fa + d
+                    b = states[2 * h + 1] * fb + d
+                    states[2 * h : 2 * h + 2] = a, b
+                    ysum[h, pl.ds(pl.multiple_of((base + t) * 8, 8), 8), :] = a * sa + b * sb
+            return tuple(states)
+
+        lax.fori_loop(0, TOK // 8, one, tuple(starts))
+        for h in range(2):
+            total = ysum[h, pl.ds(0, TOK, stride=8), :]
+            for i in range(1, 8):
+                total += ysum[h, pl.ds(i, TOK, stride=8), :]
+            conv[h] = total + skip_ref[:, lanes(h)] * drive[h]
 
     def finish(h):
         stops = (HALF - h, HALF - 1 + h)
@@ -388,9 +394,7 @@
             b_own()
         if step == HALF + 2:
             take(est.at[pl.ds(0, Z - 1)], e_r.at[0])
-            part3(0)
-        if step == HALF + 3:
-            part3(1)
+            part3()
     finish(0)
     finish(1)
     for ref, sem in sent:
@@ -425,7 +429,7 @@
             pltpu.VMEM((2, TOK, LANE), f32),
             pltpu.VMEM((Z, 2, MODES, LANE), bf16),
             pltpu.VMEM((MODES, LANE), f32),
-            pltpu.VMEM((TOK * 8, LANE), f32),
+            pltpu.VMEM((2, TOK * 8, LANE), f32),
             dma((6,)), dma((1,)), dma((1,)), dma((n,)), dma((n,)), dma((n,)), dma((n,)),
             dma((n,)), dma((n,)),
             dma((2, 2, 2)), dma((2, 2, HALF, 2)), dma((2, 2, 2)), dma((2, 2, HALF, 2)),

time: 114 us -> 113 us (level)
  no operation moved by 1% of the time
where the time goes in v7:
time: 113 us; the launch traced here: 112 us
  Pallas kernels  111 us (98%)
  local copies, waits for them, and re-layouts  1.57 us (1%)
    pallas_call x1, Pallas kernels, per_device(): pl.pallas_call(kernel, out_shape=jax.ShapeDtypeStruct(inputs.shape, jnp.b...  111 us

profile of v7, /device:TPU:24, one launch (start us, length us, event | category | flops | bytes accessed | tf_op | source)
XLA Modules:
  0.0 112.3 jit_solution(9625881710877789827)
XLA Ops:
  0.0 110.8 %shard_map.64 = bf16[256,256]{1,0:T(8,128)(2,1)} custom-call(bf16[256,256]{1,0:T(8,128)(2,1)} %x_hbm.1, bf16[3,512,256]{2,1,0:T(8,128)(2,1)} %w_hbm.1, f32[3,3,256]{2,1,0:T(4,128)} %sf_hbm.1, f32[16,256]{1,0:T(8,128)} %rates_hbm.1, f32[16,256]{1,0:T(8,128)} %res_hbm.1, f32[1,256]{1,0:T(1,128)} %bitcast.1), custom_call_target="tpu_custom_call" | custom-call | tf_op jit(solution)/shard_map/pallas_call | solution.py:409
  110.8 1.6 %copy.8 = bf16[256,256]{1,0:T(8,128)(2,1)} copy(bf16[256,256]{1,0:T(8,128)(2,1)} %shard_map.64) | data formatting | bytes 262144
